TPU v7x, 32 devices: a whole 2x2x4 slice. The times are simulated.
32 devices in a mesh: segment: 4 (over z), seq: 8 (over y, x, core).
Axes of the slice: x: 2, y: 2, z: 4, core: 2. Of those that a mesh axis runs over, the one named last changes fastest.
Arguments:
- queries: bfloat16 [4, 4096, 8192], P('segment', 'seq'), may hold values from -40 to 40
- keys_in: bfloat16 [4, 4096, 1024], P('segment', 'seq'), may hold values from -6 to 6
- values_in: bfloat16 [4, 4096, 1024], P('segment', 'seq'), may hold values from -6 to 6
- random_blocks: int32 [4, 64, 3], P('segment', 'seq'), may hold values from 0 to 63, as said below
- global_blocks: int32 [4, 2], P('segment'), may hold values from 0 to 63
Outputs:
- handed: bfloat16 [4, 4096, 8192], P('segment', 'seq')
Inputs may be any that keep to these rules, and one draw needn't show every extreme that they name: random_blocks[s, j] are block numbers; the rows of one device of seq name at most 3 blocks lying on any single device of seq, and in every section one device of seq is named exactly once by the rows of every device.
All inputs are finite; a program needn't handle non-finite values.
Results may differ from a plain program's by a relative error of at most 0.0049.
Values may be sent and summed in bfloat16 or wider, within the bound.
A program may use at most 128 MiB of HBM per device.

v0:
```python
import jax
import jax.numpy as jnp
from jax import lax
from jax.sharding import PartitionSpec as P

HEAD = 128
BLOCK = 64
GLOB = 2
RAND = 3


def padded_2(x, sides, width):
    for axis, dim in sides:
        size, length = (lax.axis_size(axis), x.shape[dim])
        up = [(i, (i + 1) % size) for i in range(size - 1)]
        down = [(j, i) for i, j in up]
        last = lax.slice_in_dim(x, length - width, length, axis=dim)
        leading = lax.slice_in_dim(x, 0, width, axis=dim)
        before = lax.ppermute(last, axis, up)
        after = lax.ppermute(leading, axis, down)
        x = jnp.concatenate([before, x, after], axis=dim)
    return x


def shifted(x, axis, by):
    length = lax.axis_size(axis)
    return lax.ppermute(x, axis, [(i, (i + by) % length) for i in range(length)])


def slot_table(owners, local, ranks, number_of_strings, cap):
    match_owner = (
        owners[None, None, :] == jnp.arange(number_of_strings, dtype=jnp.int32)[:, None, None]
    )
    match_rank = ranks[None, None, :] == jnp.arange(cap, dtype=jnp.int32)[None, :, None]
    picked = jnp.where(match_owner & match_rank & True, local[None, None, :], 0)
    return jnp.sum(picked, axis=-1)


def rank_among(owners):
    count = owners.shape[0]
    same = owners[:, None] == owners[None, :]
    earlier = jnp.arange(count)[None, :] < jnp.arange(count)[:, None]
    return jnp.sum(same & earlier, axis=1)


def per_device(queries, keys_in, values_in, random_blocks, global_blocks):
    tok = queries.shape[1]
    kvw = keys_in.shape[2]
    kvh = kvw // HEAD
    group = queries.shape[2] // kvw
    blk_dev = tok // BLOCK
    number_of_strings = lax.axis_size("seq")
    me = lax.axis_index("seq")
    nblk = blk_dev * number_of_strings
    wanted = blk_dev * RAND
    cap = max(1, (wanted + number_of_strings - 1) // number_of_strings)
    width = 2 * kvw
    joined = jnp.concatenate([keys_in[0], values_in[0]], axis=-1)
    local_blocks = joined.reshape(blk_dev, BLOCK, width)
    padded = padded_2(joined, (("seq", 0),), BLOCK)
    padded_blocks = padded.reshape(blk_dev + 2, BLOCK, width)
    window = jnp.stack([padded_blocks[:-2], padded_blocks[1:-1], padded_blocks[2:]], axis=1)
    global_row = global_blocks[0]
    offset = global_row - me * blk_dev
    mine = (offset >= 0) & (offset < blk_dev)
    chosen = local_blocks[jnp.clip(offset, 0, blk_dev - 1)]
    contrib = jnp.where(mine[:, None, None], chosen.astype(jnp.float32), 0.0)
    global_kv = lax.psum(contrib.astype(jnp.bfloat16), "seq")
    requests = random_blocks[0].reshape(wanted)
    owners = requests // blk_dev
    local = requests % blk_dev
    ranks = rank_among(owners)
    table = slot_table(owners, local, ranks, number_of_strings, cap)
    asked = lax.all_to_all(table, "seq", split_axis=0, concat_axis=0, tiled=True)
    outgoing = local_blocks[asked.reshape(number_of_strings * cap)].reshape(
        number_of_strings, cap, BLOCK, width
    )
    incoming = lax.all_to_all(outgoing, "seq", split_axis=0, concat_axis=0, tiled=True)
    fetched = incoming.reshape(number_of_strings * cap, BLOCK, width)[owners * cap + ranks]
    fetched = fetched.reshape(blk_dev, RAND, BLOCK, width)
    global_wide = jnp.broadcast_to(global_kv[None], (blk_dev, GLOB, BLOCK, width))
    all_keys = jnp.concatenate([window, global_wide, fetched], axis=1)
    keys_total = all_keys.shape[1] * BLOCK
    all_keys = all_keys.reshape(blk_dev, keys_total, width)
    rows_global = me * blk_dev + jnp.arange(blk_dev, dtype=jnp.int32)
    valid = jnp.concatenate(
        [
            (rows_global >= 1)[:, None],
            jnp.ones((blk_dev, 1), bool),
            (rows_global + 1 < nblk)[:, None],
            jnp.ones((blk_dev, GLOB + RAND), bool),
        ],
        axis=1,
    )
    mask = jnp.repeat(valid, BLOCK, axis=1)
    query_blocks = queries[0].reshape(blk_dev, BLOCK, kvh, group, HEAD)
    scale = 1.0 / HEAD**0.5
    results = []
    for head_kv in range(kvh):
        query_portion = query_blocks[:, :, head_kv]
        key_portion = all_keys[:, :, head_kv * HEAD : (head_kv + 1) * HEAD]
        value_portion = all_keys[:, :, kvw + head_kv * HEAD : kvw + (head_kv + 1) * HEAD]
        scores = (
            jnp.einsum(
                "uoic,ufc->uiof", query_portion, key_portion, preferred_element_type=jnp.float32
            )
            * scale
        )
        scores = jnp.where(mask[:, None, None, :], scores, -jnp.inf)
        top = jnp.max(scores, axis=-1, keepdims=True)
        expo = jnp.exp(scores - top)
        attention_probs = (expo / jnp.sum(expo, axis=-1, keepdims=True)).astype(jnp.bfloat16)
        result = jnp.einsum(
            "xuys,xsi->xyui", attention_probs, value_portion, preferred_element_type=jnp.float32
        )
        result = result.astype(jnp.bfloat16).reshape(tok, group * HEAD)
        results.append(result[None])
    combined = jnp.concatenate(results, axis=-1)
    combined = shifted(combined, "segment", 1)
    return combined


def solution(mesh):
    in_specs = (
        P("segment", "seq", None),
        P("segment", "seq", None),
        P("segment", "seq", None),
        P("segment", "seq", None),
        P("segment", None),
    )
    out_specs = P("segment", "seq", None)
    return jax.shard_map(
        per_device, mesh=mesh, in_specs=in_specs, out_specs=out_specs, check_vma=False
    )
```

profile of v0, /device:TPU:0, one launch (start us, length us, event | category | flops | bytes accessed | tf_op | source)
XLA Modules:
  0.0 448.2 jit_solution(11811748637419781580)
XLA Ops:
  8.4 5.2 %all-to-all-start = ((s32[8,1,3]{2,1,0:T(1,128)}), s32[8,1,3]{2,1,0:T(1,128)S(1)}, u32[]{:S(2)}, u32[]{:S(2)}) async-start(s32[8,1,3]{2,1,0:T(1,128)} %copy.62), calls=%async_computation | async-start | bytes 8192 | tf_op jit(solution)/shard_map/all_to_all | solution.py:74
  19.5 4.4 gather_fusion.1
  23.8 4.9 %all-to-all-start.1 = ((bf16[8,3,64,2048]{3,2,1,0:T(8,128)(2,1)}), bf16[8,3,64,2048]{3,2,1,0:T(8,128)(2,1)}, u32[]{:S(2)}, u32[]{:S(2)}) async-start(bf16[8,3,64,2048]{3,2,1,0:T(8,128)(2,1)} %bitcast.265), calls=%async_computation.1 | async-start | bytes 12582912 | tf_op jit(solution)/shard_map/all_to_all | solution.py:78
  34.8 9.5 %copy.106 = bf16[64,8,64,128]{3,2,1,0:T(8,128)(2,1)} copy(bf16[64,8,64,128]{3,1,2,0:T(8,128)(2,1)} %bitcast.275) | data formatting | bytes 16777216
  44.7 6.9 %fusion.117 = (bf16[8,64,1,8,128]{4,3,2,1,0:T(8,128)(2,1)}, bf16[8,64,1,8,128]{4,3,2,1,0:T(8,128)(2,1)}, bf16[8,64,1,8,128]{4,3,2,1,0:T(8,128)(2,1)}, bf16[8,64,...) fusion(bf16[8,64,8,8,128]{4,3,2,1,0:T(8,128)(2,1)} %bitcast.264), kind=kLoop, calls=%fused_computation.206 | loop fusion | bytes 16777216 | tf_op jit(solution)/shard_map/slice | solution.py:100
  55.2 5.0 %pad_maximum_fusion = (bf16[512,2048]{1,0:T(8,128)(2,1)S(1)}, bf16[512,2048]{1,0:T(8,128)(2,1)S(1)}) fusion(bf16[64,2048]{1,0:T(8,128)(2,1)} %collective-permute-done.1, bf16[512,1024]{1,0:T(8,128)(2,1)S(1)} %bitcast.269, bf16[512,1024]{1,0:T(8,128)(2,1)} %bitcast.273, bf16[64,2048]{1,0:T(8,128)(2,1)} %collective-permute-done), kind=kLoop, calls=%fused_computation.91 | loop fusion | flops 12582912 | bytes 6815744 | tf_op jit(solution)/shard_map/concatenate | solution.py:21
  64.8 64.5 %all-reduce.2.cloned.1.call-done = bf16[2,64,2048]{2,1,0:T(8,128)(2,1)} async-done(((bf16[2,64,2048]{2,1,0:T(8,128)(2,1)}), bf16[2,64,2048]{2,1,0:T(8,128)(2,1)}) %all-reduce.2.cloned.1.call-update) | async-done | bytes 524304 | tf_op jit(solution)/shard_map/psum | solution.py:68
  129.2 3.5 broadcast_dynamic-update-slice_fusion
  132.7 7.3 %gather_fusion.2 = bf16[24,64,2048]{2,1,0:T(8,128)(2,1)} fusion(bf16[24,64,2048]{2,1,0:T(8,128)(2,1)} %bitcast.18, s32[1024]{0:T(1024)S(1)} %pad_clamp_fusion), kind=kCustom, calls=%fused_computation.2 | custom fusion | bytes 12583008 | tf_op jit(solution)/shard_map/gather | solution.py:79
  140.0 6.6 %constant_dynamic-update-slice_fusion = bf16[8,8,64,2048]{3,2,1,0:T(8,128)(2,1)} fusion(bf16[8,8,64,2048]{3,2,1,0:T(8,128)(2,1)} %broadcast_dynamic-update-slice_fusion, bf16[8,3,64,2048]{3,2,1,0:T(8,128)(2,1)} %bitcast.266), kind=kLoop, calls=%fused_computation.149 | loop fusion | bytes 12582912 | tf_op jit(solution)/shard_map/concatenate | solution.py:82
  149.1 3.1 fusion.125
  158.9 3.1 fusion.124
  170.9 3.1 fusion.123
  174.1 3.0 fusion.85
  183.5 3.1 fusion.122
  196.2 3.1 fusion.121
  199.3 3.0 fusion.83
  208.8 3.1 fusion.120
  211.9 3.2 fusion.82
  221.6 3.1 fusion.119
  224.8 3.0 fusion.81
  234.2 3.1 fusion.118
  251.5 181.7 %collective-permute-done.2 = bf16[1,512,8192]{2,1,0:T(8,128)(2,1)} collective-permute-done((bf16[1,512,8192]{2,1,0:T(8,128)(2,1)S(1)}, bf16[1,512,8192]{2,1,0:T(8,128)(2,1)}, u32[]{:S(2)}, u32[]{:S(2)}) %collective-permute-start.2) | collective-permute-done | bytes 8388640 | tf_op jit(solution)/shard_map/ppermute | solution.py:27
  433.2 7.8 %copy.136 = bf16[1,512,8192]{2,1,0:T(8,128)(2,1)} copy(bf16[1,512,8192]{2,1,0:T(8,128)(2,1)} %collective-permute-done.2) | data formatting | bytes 16777216
  (103 shorter events, 89.7 us)
Async XLA Ops:
  8.4 9.8 %all-to-all-start = ((s32[8,1,3]{2,1,0:T(1,128)}), s32[8,1,3]{2,1,0:T(1,128)S(1)}, u32[]{:S(2)}, u32[]{:S(2)}) async-start(s32[8,1,3]{2,1,0:T(1,128)} %copy.62), calls=%async_computation | async-start | bytes 8192 | tf_op jit(solution)/shard_map/all_to_all | solution.py:74
  23.8 4.9 %copy-start = (bf16[1,512,1024]{2,1,0:T(8,128)(2,1)S(1)}, bf16[1,512,1024]{2,1,0:T(8,128)(2,1)}, u32[]{:S(2)}) copy-start(bf16[1,512,1024]{2,1,0:T(8,128)(2,1)} %param.7) | copy-start | bytes 3145732
  23.8 108.9 %all-to-all-start.1 = ((bf16[8,3,64,2048]{3,2,1,0:T(8,128)(2,1)}), bf16[8,3,64,2048]{3,2,1,0:T(8,128)(2,1)}, u32[]{:S(2)}, u32[]{:S(2)}) async-start(bf16[8,3,64,2048]{3,2,1,0:T(8,128)(2,1)} %bitcast.265), calls=%async_computation.1 | async-start | bytes 12582912 | tf_op jit(solution)/shard_map/all_to_all | solution.py:78
  28.7 100.5 %all-reduce.2.cloned.1.call-start = ((), (), s32[]{:S(2)}) async-start(), calls=%async_computation.2 | async-start | bytes 1048576 | tf_op jit(solution)/shard_map/psum | solution.py:68
  30.5 24.7 %collective-permute-start = (bf16[64,2048]{1,0:T(8,128)(2,1)}, bf16[64,2048]{1,0:T(8,128)(2,1)}, u32[]{:S(2)}, u32[]{:S(2)}) collective-permute-start(bf16[64,2048]{1,0:T(8,128)(2,1)} %get-tuple-element.16), channel_id=1, source_target_pairs={{0,1},{1,2},{2,3},{3,4},{4,5},{5,6},{6,7},{8,9},{9,10},{10,11},{11... | collective-permute-start | bytes 786440 | tf_op jit(solution)/shard_map/ppermute | solution.py:19
  33.4 21.8 %collective-permute-start.1 = (bf16[64,2048]{1,0:T(8,128)(2,1)S(1)}, bf16[64,2048]{1,0:T(8,128)(2,1)}, u32[]{:S(2)}, u32[]{:S(2)}) collective-permute-start(bf16[64,2048]{1,0:T(8,128)(2,1)S(1)} %get-tuple-element.15), channel_id=1, source_target_pairs={{1,0},{2,1},{3,2},{4,3},{5,4},{6,5},{7,6},{9,8},{10,9},{11,10},{12... | collective-permute-start | bytes 786440 | tf_op jit(solution)/shard_map/ppermute | solution.py:20
  34.8 10.0 %copy-start.12 = (s32[1,2]{1,0:T(1,128)S(1)}, s32[1,2]{1,0:T(1,128)}, u32[]{:S(2)}) copy-start(s32[1,2]{1,0:T(1,128)} %param.9) | copy-start | bytes 28
  53.0 8.7 %copy-start.1 = (bf16[1,512,1024]{2,1,0:T(8,128)(2,1)S(1)}, bf16[1,512,1024]{2,1,0:T(8,128)(2,1)}, u32[]{:S(2)}) copy-start(bf16[1,512,1024]{2,1,0:T(8,128)(2,1)} %param.6) | copy-start | bytes 3145732
  140.0 6.6 %copy-start.9 = (bf16[8,64,1,8,128]{4,3,2,1,0:T(8,128)(2,1)S(1)}, bf16[8,64,1,8,128]{4,3,2,1,0:T(8,128)(2,1)}, u32[]{:S(2)}) copy-start(bf16[8,64,1,8,128]{4,3,2,1,0:T(8,128)(2,1)} %get-tuple-element.5) | copy-start | bytes 3145732
  152.2 4.2 copy-start.8
  162.0 6.4 %copy-start.7 = (bf16[8,64,1,8,128]{4,3,2,1,0:T(8,128)(2,1)S(1)}, bf16[8,64,1,8,128]{4,3,2,1,0:T(8,128)(2,1)}, u32[]{:S(2)}) copy-start(bf16[8,64,1,8,128]{4,3,2,1,0:T(8,128)(2,1)} %get-tuple-element.7) | copy-start | bytes 3145732
  174.1 7.0 %copy-start.6 = (bf16[8,64,1,8,128]{4,3,2,1,0:T(8,128)(2,1)S(1)}, bf16[8,64,1,8,128]{4,3,2,1,0:T(8,128)(2,1)}, u32[]{:S(2)}) copy-start(bf16[8,64,1,8,128]{4,3,2,1,0:T(8,128)(2,1)} %get-tuple-element.8) | copy-start | bytes 3145732
  186.7 7.0 %copy-start.5 = (bf16[8,64,1,8,128]{4,3,2,1,0:T(8,128)(2,1)S(1)}, bf16[8,64,1,8,128]{4,3,2,1,0:T(8,128)(2,1)}, u32[]{:S(2)}) copy-start(bf16[8,64,1,8,128]{4,3,2,1,0:T(8,128)(2,1)} %get-tuple-element.9) | copy-start | bytes 3145732
  199.3 7.0 %copy-start.4 = (bf16[8,64,1,8,128]{4,3,2,1,0:T(8,128)(2,1)S(1)}, bf16[8,64,1,8,128]{4,3,2,1,0:T(8,128)(2,1)}, u32[]{:S(2)}) copy-start(bf16[8,64,1,8,128]{4,3,2,1,0:T(8,128)(2,1)} %get-tuple-element.10) | copy-start | bytes 3145732
  211.9 7.2 %copy-start.3 = (bf16[8,64,1,8,128]{4,3,2,1,0:T(8,128)(2,1)S(1)}, bf16[8,64,1,8,128]{4,3,2,1,0:T(8,128)(2,1)}, u32[]{:S(2)}) copy-start(bf16[8,64,1,8,128]{4,3,2,1,0:T(8,128)(2,1)} %get-tuple-element.11) | copy-start | bytes 3145732
  224.7 7.0 %copy-start.2 = (bf16[8,64,1,8,128]{4,3,2,1,0:T(8,128)(2,1)S(1)}, bf16[8,64,1,8,128]{4,3,2,1,0:T(8,128)(2,1)}, u32[]{:S(2)}) copy-start(bf16[8,64,1,8,128]{4,3,2,1,0:T(8,128)(2,1)} %get-tuple-element.12) | copy-start | bytes 3145732
  240.2 9.5 %copy-start.10 = (bf16[1,512,1024]{2,1,0:T(8,128)(2,1)S(1)}, bf16[1,512,1024]{2,1,0:T(8,128)(2,1)}, u32[]{:S(2)}) copy-start(bf16[1,512,1024]{2,1,0:T(8,128)(2,1)} %broadcast_in_dim_reshape.37) | copy-start | bytes 3145732
  244.3 5.4 %copy-start.11 = (bf16[1,512,1024]{2,1,0:T(8,128)(2,1)S(1)}, bf16[1,512,1024]{2,1,0:T(8,128)(2,1)}, u32[]{:S(2)}) copy-start(bf16[1,512,1024]{2,1,0:T(8,128)(2,1)} %broadcast_in_dim_reshape.36) | copy-start | bytes 3145732
  250.0 183.2 %collective-permute-start.2 = (bf16[1,512,8192]{2,1,0:T(8,128)(2,1)S(1)}, bf16[1,512,8192]{2,1,0:T(8,128)(2,1)}, u32[]{:S(2)}, u32[]{:S(2)}) collective-permute-start(bf16[1,512,8192]{2,1,0:T(8,128)(2,1)S(1)} %constant_dynamic-update-slice_fusion.3), channel_id=1, source_target_pairs={{0,8},{8,16},{16,24},{24,0},{1,9},{9,17},{17,25},{25,1},{2,10},{10... | collective-permute-start | bytes 25165832 | tf_op jit(solution)/shard_map/ppermute | solution.py:27
Sparse Core Ops, SparseCore 0:
  55.3 73.9 all-reduce.1
where the time goes:
time: 453 us; the launch traced here: 448 us
  waiting for transfers between devices  248 us (55%)
  local copies, waits for them, and re-layouts  87.3 us (19%)
  matrix products  43.6 us (10%)
  other arithmetic  38.9 us (9%)
  starting transfers between devices  15.8 us (3%)
  between operations  14.3 us (3%)
    ppermute x1, waiting for transfers between devices, shifted(): lax.ppermute(x, axis, [(i, (i + by) % length) for i in range(length)])  182 us
    psum x1, waiting for transfers between devices, per_device(): global_kv = lax.psum(contrib.astype(jnp.bfloat16), 'seq')  64.5 us
    unnamed x39, local copies, waits for them, and re-layouts  30.3 us
    sub x8, other arithmetic, per_device(): expo = jnp.exp(scores - top)  25.1 us
    dot_general x8, matrix products, per_device(): jnp.einsum('xuys,xsi->xyui', attention_probs, value_portion, preferred_el...  23.8 us
    dot_general x8, matrix products, per_device(): jnp.einsum('uoic,ufc->uiof', query_portion, key_portion, preferred_elemen...  19.8 us
    another operation x8, local copies, waits for them, and re-layouts, per_device(): results.append(result[None])  16.1 us
    convert_element_type x8, local copies, waits for them, and re-layouts, per_device(): result = result.astype(jnp.bfloat16).reshape(tok, group * HEAD)  12.6 us
  transfers between devices with their start and end apart: 6, of which 3 were waited for; matrix products, arithmetic and copies ran while one was open for 8% of the time, Pallas kernels for 0%

commit v1 on v0

v1 whole, which is shorter than its diff:
```python
import functools
import math

import jax
import jax.numpy as jnp
from jax import lax
from jax.experimental import pallas as pl
from jax.experimental.pallas import tpu as pltpu
from jax.sharding import PartitionSpec as P

HEAD = 128
BLOCK = 64
GLOB = 2
RAND = 3
MESH = pl.DeviceIdType.MESH
SLOT_BYTES = 16 * 1024 * 1024


def kernel(
    n, segs, kvh, slots, ahead,
    rand_ref, glob_ref, q_ref, k_ref, v_ref, out_ref,
    q_buf, res, *rest,
):
    kv = rest[:slots]
    q_sem, own_sem, send_sem, recv_sem, fsend, frecv, zsend, zrecv, free_c, free_p = rest[slots:]
    tok = q_ref.shape[1]
    group = q_ref.shape[2] // (kvh * HEAD)
    gw = group * HEAD
    blk_dev = tok // BLOCK
    nblk = blk_dev * n
    chips = n // 2
    me = lax.axis_index("seq")
    seg = lax.axis_index("segment")
    chip, core = me // 2, me % 2
    partner = chip * 2 + (1 - core)
    after, before = (seg + 1) % segs, (seg + segs - 1) % segs
    others = [(chip + o) % chips for o in range(1, chips)]

    def q_copy(h):
        return pltpu.make_async_copy(
            q_ref.at[0, :, pl.ds(h * gw, gw)], q_buf.at[h], q_sem.at[h]
        )

    def place(s, c, i):
        return kv[s].at[pl.ds((core * 2 + i) * chips * blk_dev + c * blk_dev, blk_dev)]

    def own_copy(h, i):
        src = (k_ref, v_ref)[i].at[:, :, pl.ds(h * HEAD, HEAD)]
        return pltpu.make_async_copy(src, place(h % slots, chip, i), own_sem.at[h % slots, i])

    def peer_copy(h, c, i):
        s = h % slots
        src = (k_ref, v_ref)[i].at[:, :, pl.ds(h * HEAD, HEAD)]
        return pltpu.make_async_remote_copy(
            src_ref=src, dst_ref=place(s, chip, i),
            send_sem=send_sem.at[s, c, i], recv_sem=recv_sem.at[s, chip, i],
            device_id={"seq": c * 2 + core}, device_id_type=MESH,
        )

    def peer_arrival(h, c, i):
        s = h % slots
        src = (k_ref, v_ref)[i].at[:, :, pl.ds(h * HEAD, HEAD)]
        return pltpu.make_async_remote_copy(
            src_ref=src, dst_ref=place(s, c, i),
            send_sem=send_sem.at[s, c, i], recv_sem=recv_sem.at[s, c, i],
            device_id={"seq": c * 2 + core}, device_id_type=MESH,
        )

    def forward(h, half):
        s = h % slots
        part = kv[s].at[pl.ds(half * 2 * chips * blk_dev, 2 * chips * blk_dev)]
        return pltpu.make_async_remote_copy(
            src_ref=part, dst_ref=part,
            send_sem=fsend.at[s], recv_sem=frecv.at[s],
            device_id={"seq": partner}, device_id_type=MESH,
        )

    def start_gather(h):
        if h >= slots:
            pl.semaphore_wait(free_c.at[h % slots], chips - 1)
        for i in range(2):
            for c in others:
                peer_copy(h, c, i).start()
            own_copy(h, i).start()

    barrier = pltpu.get_barrier_semaphore()
    greeted = [{"seq": c * 2 + core} for c in others]
    greeted += [{"seq": partner}, {"segment": after}, {"segment": before}]
    for who in greeted:
        pl.semaphore_signal(barrier, inc=1, device_id=who, device_id_type=MESH)
    q_copy(0).start()
    pl.semaphore_wait(barrier, len(greeted))

    for h in range(min(ahead, slots, kvh)):
        start_gather(h)
    for h in range(1, kvh):
        q_copy(h).start()

    scale = 1.0 / math.sqrt(HEAD)
    column = lax.broadcasted_iota(jnp.int32, (1, (3 + GLOB + RAND) * BLOCK), 1)

    for h in range(kvh):
        s = h % slots
        for i in range(2):
            own_copy(h, i).wait()
            for c in others:
                peer_arrival(h, c, i).wait_recv()
        if h >= slots:
            pl.semaphore_wait(free_p.at[s], 1)
        forward(h, core).start()
        if ahead <= slots and h + ahead < kvh and h + ahead < slots:
            start_gather(h + ahead)
        q_copy(h).wait()
        forward(h, 1 - core).wait_recv()

        def block_step(j, carry, h=h, s=s):
            row = me * blk_dev + j
            listed = [jnp.maximum(row - 1, 0), row, jnp.minimum(row + 1, nblk - 1)]
            listed += [glob_ref[0, i] for i in range(GLOB)]
            listed += [rand_ref[0, j, i] for i in range(RAND)]

            def picked(i):
                parts = []
                for b in listed:
                    dev = lax.div(b, blk_dev)
                    where = (lax.rem(dev, 2) * 2 + i) * chips + lax.div(dev, 2)
                    parts.append(kv[s][where * blk_dev + lax.rem(b, blk_dev)])
                return jnp.concatenate(parts, axis=0)

            rows = pl.ds(pl.multiple_of(j * BLOCK, BLOCK), BLOCK)
            q_rows = q_buf[h, rows, :]
            q = jnp.concatenate([q_rows[:, g * HEAD : (g + 1) * HEAD] for g in range(group)], axis=0)
            scores = lax.dot_general(
                q, picked(0), (((1,), (1,)), ((), ())), preferred_element_type=jnp.float32
            )
            listed_here = ((column >= BLOCK) | (row >= 1)) & (
                (column < 2 * BLOCK) | (column >= 3 * BLOCK) | (row + 1 < nblk)
            )
            scores = scores * scale + jnp.where(listed_here, 0.0, -jnp.inf)
            top = jnp.max(scores, axis=-1, keepdims=True)
            expo = jnp.exp(scores - top)
            weights = (expo * (1.0 / jnp.sum(expo, axis=-1, keepdims=True))).astype(jnp.bfloat16)
            result = jnp.dot(weights, picked(1), preferred_element_type=jnp.float32)
            result = result.astype(jnp.bfloat16)
            for g in range(group):
                res[h, rows, pl.ds(g * HEAD, HEAD)] = result[g * BLOCK : (g + 1) * BLOCK, :]
            pltpu.make_async_remote_copy(
                src_ref=res.at[h, rows, :],
                dst_ref=out_ref.at[0, rows, pl.ds(h * gw, gw)],
                send_sem=zsend.at[h], recv_sem=zrecv.at[h],
                device_id={"segment": after}, device_id_type=MESH,
            ).start()
            return carry

        lax.fori_loop(0, blk_dev, block_step, 0)

        for i in range(2):
            for c in others:
                peer_copy(h, c, i).wait_send()
        forward(h, core).wait_send()
        if h + slots < kvh:
            for c in others:
                pl.semaphore_signal(
                    free_c.at[s], inc=1, device_id={"seq": c * 2 + core}, device_id_type=MESH
                )
            pl.semaphore_signal(
                free_p.at[s], inc=1, device_id={"seq": partner}, device_id_type=MESH
            )
            start_gather(h + slots)

    for h in range(kvh):
        pltpu.make_async_remote_copy(
            src_ref=res.at[h],
            dst_ref=out_ref.at[0, :, pl.ds(h * gw, gw)],
            send_sem=zsend.at[h], recv_sem=zrecv.at[h],
            device_id={"segment": after}, device_id_type=MESH,
        ).wait()


def per_device(queries, keys_in, values_in, random_blocks, global_blocks):
    n, segs = lax.axis_size("seq"), lax.axis_size("segment")
    tok, width = queries.shape[1:]
    kvh = keys_in.shape[2] // HEAD
    gw = width // kvh
    chips = n // 2
    slots = min(kvh, max(2, SLOT_BYTES // (4 * n * tok * HEAD)))
    anywhere = pl.BlockSpec(memory_space=pl.ANY)
    scalars = pl.BlockSpec(memory_space=pltpu.SMEM)
    keys = (3 + GLOB + RAND) * BLOCK
    keys_in, values_in = (x.reshape(tok // BLOCK, BLOCK, kvh * HEAD) for x in (keys_in, values_in))
    return pl.pallas_call(
        functools.partial(kernel, n, segs, kvh, slots, min(2, slots)),
        out_shape=jax.ShapeDtypeStruct(queries.shape, jnp.bfloat16),
        in_specs=[scalars, scalars, anywhere, anywhere, anywhere],
        out_specs=anywhere,
        scratch_shapes=[
            pltpu.VMEM((kvh, tok, gw), jnp.bfloat16),
            pltpu.VMEM((kvh, tok, gw), jnp.bfloat16),
            *[pltpu.VMEM((4 * chips * tok // BLOCK, BLOCK, HEAD), jnp.bfloat16) for _ in range(slots)],
            pltpu.SemaphoreType.DMA((kvh,)),
            pltpu.SemaphoreType.DMA((slots, 2)),
            pltpu.SemaphoreType.DMA((slots, chips, 2)),
            pltpu.SemaphoreType.DMA((slots, chips, 2)),
            pltpu.SemaphoreType.DMA((slots,)),
            pltpu.SemaphoreType.DMA((slots,)),
            pltpu.SemaphoreType.DMA((kvh,)),
            pltpu.SemaphoreType.DMA((kvh,)),
            pltpu.SemaphoreType.REGULAR((slots,)),
            pltpu.SemaphoreType.REGULAR((slots,)),
        ],
        compiler_params=pltpu.CompilerParams(
            collective_id=0, has_side_effects=True, vmem_limit_bytes=56 * 1024 * 1024
        ),
        cost_estimate=pl.CostEstimate(
            flops=4 * tok * width * keys,
            bytes_accessed=4 * tok * width,
            transcendentals=tok * width // HEAD * keys,
        ),
    )(random_blocks, global_blocks, queries, keys_in, values_in)


def solution(mesh):
    in_specs = (
        P("segment", "seq", None),
        P("segment", "seq", None),
        P("segment", "seq", None),
        P("segment", "seq", None),
        P("segment", None),
    )
    out_specs = P("segment", "seq", None)
    return jax.shard_map(
        per_device, mesh=mesh, in_specs=in_specs, out_specs=out_specs, check_vma=False
    )
```

time: 453 us -> 216 us (0.48)
  waiting for transfers between devices: 248 us -> 0 us
  Pallas kernels: 0 us -> 205 us
  local copies, waits for them, and re-layouts: 87.3 us -> 9.12 us
  matrix products: 43.6 us -> 0 us
  other arithmetic: 38.9 us -> 0 us
  starting transfers between devices: 15.8 us -> 0 us
  between operations: 14.3 us -> 0.01 us
    pallas_call x0 -> x1, Pallas kernels: none -> 205 us  [per_device(): pl.pallas_call(functools.partial(kernel, n, segs, kvh, slots, min(2, slot...]
    ppermute x3 -> x0, waiting for transfers between devices: 182 us -> none  [the longest x1 182 us: shifted(): lax.ppermute(x, axis, [(i, (i + by) % length) for i in range(length)])]
    psum x1 -> x0, waiting for transfers between devices: 64.5 us -> none  [per_device(): global_kv = lax.psum(contrib.astype(jnp.bfloat16), 'seq')]
    dot_general x16 -> x0, matrix products: 43.6 us -> none  [the longest x8 23.8 us: per_device(): jnp.einsum('xuys,xsi->xyui', attention_probs, value_portion, preferred_el...]
    sub x8 -> x0, other arithmetic: 25.1 us -> none  [per_device(): expo = jnp.exp(scores - top)]
    unnamed x39 -> x2, local copies, waits for them, and re-layouts: 30.3 us -> 9.12 us
    another operation x10 -> x0, local copies, waits for them, and re-layouts: 16.3 us -> none  [the longest x8 16.1 us: per_device(): results.append(result[None])]
    gather x3 -> x0, local copies, waits for them, and re-layouts: 13 us -> none  [the longest x1 7.28 us: per_device(): incoming.reshape(number_of_strings * cap, BLOCK, width)]
  transfers between devices with their start and end apart: 6 -> 0, of which waited for: 3 -> 0; matrix products, arithmetic and copies ran while one was open for 8% -> 0% of each run, Pallas kernels for 0% -> 0%
where the time goes in v1:
time: 216 us; the launch traced here: 214 us
  Pallas kernels  205 us (95%)
  local copies, waits for them, and re-layouts  9.12 us (4%)
    pallas_call x1, Pallas kernels, per_device(): pl.pallas_call(functools.partial(kernel, n, segs, kvh, slots, min(2, slot...  205 us
    unnamed x2, local copies, waits for them, and re-layouts  9.12 us

profile of v1, /device:TPU:0, one launch (start us, length us, event | category | flops | bytes accessed | tf_op | source)
XLA Modules:
  0.0 214.4 jit_solution(912971287947803563)
XLA Ops:
  0.0 1.3 copy.6.rand_ref
  1.3 205.3 %shard_map.55 = bf16[1,512,8192]{2,1,0:T(8,128)(2,1)} custom-call(s32[1,8,3]{2,1,0:T(8,128)} %copy.6.rand_ref, s32[1,2]{1,0:T(1,128)} %glob_ref.1, bf16[1,512,8192]{2,1,0:T(8,128)(2,1)} %q_ref.1, bf16[8,64,1024]{2,1,0:T(8,128)(2,1)} %bitcast.2, bf16[8,64,1024]{2,1,0:T(8,128)(2,1)} %bitcast.3), custom_call_target="tpu_custom_call" | custom-call | flops 8589934592 | bytes 16777216 | tf_op jit(solution)/shard_map/pallas_call | solution.py:191
  206.6 7.8 %copy.8 = bf16[1,512,8192]{2,1,0:T(8,128)(2,1)} copy(bf16[1,512,8192]{2,1,0:T(8,128)(2,1)} %shard_map.55) | data formatting | bytes 16777216

commit v2 on v1

v2 whole, which is shorter than its diff:
```python
import functools
import math

import jax
import jax.numpy as jnp
from jax import lax
from jax.experimental import pallas as pl
from jax.experimental.pallas import tpu as pltpu
from jax.sharding import PartitionSpec as P

HEAD = 128
BLOCK = 64
GLOB = 2
RAND = 3
MESH = pl.DeviceIdType.MESH
SLOT_BYTES = 16 * 1024 * 1024


def kernel(
    n, segs, kvh, slots, ahead,
    rand_ref, glob_ref, rand_hbm, glob_hbm, q_ref, k_ref, v_ref, out_ref,
    q_buf, res, rand_in, glob_in, rand_moved, glob_moved, *rest,
):
    kv = rest[: slots + 1]
    (
        q_sem, own_sem, send_sem, recv_sem, fsend, frecv,
        zsend, zrecv, ship_send, ship_recv, table_sem, free_c, free_p,
    ) = rest[slots + 1 :]
    tok = q_ref.shape[1]
    group = q_ref.shape[2] // (kvh * HEAD)
    gw = group * HEAD
    blk_dev = tok // BLOCK
    nblk = blk_dev * n
    chips = n // 2
    moved = kvh - 1
    me = lax.axis_index("seq")
    seg = lax.axis_index("segment")
    chip, core = me // 2, me % 2
    partner = chip * 2 + (1 - core)
    after, before = (seg + 1) % segs, (seg + segs - 1) % segs
    others = [(chip + o) % chips for o in range(1, chips)]

    def slot(h):
        return slots if h == moved else h % slots

    def q_copy(h):
        return pltpu.make_async_copy(
            q_ref.at[0, :, pl.ds(h * gw, gw)], q_buf.at[h], q_sem.at[h]
        )

    def place(s, c, i):
        return kv[s].at[pl.ds((core * 2 + i) * chips * blk_dev + c * blk_dev, blk_dev)]

    def own_rows(h, i):
        return (k_ref, v_ref)[i].at[:, :, pl.ds(h * HEAD, HEAD)]

    def own_copy(h, i):
        return pltpu.make_async_copy(
            own_rows(h, i), place(slot(h), chip, i), own_sem.at[slot(h), i]
        )

    def peer_copy(h, c, i):
        s = slot(h)
        return pltpu.make_async_remote_copy(
            src_ref=place(s, chip, i) if h == moved else own_rows(h, i),
            dst_ref=place(s, chip, i),
            send_sem=send_sem.at[s, c, i], recv_sem=recv_sem.at[s, chip, i],
            device_id={"seq": c * 2 + core}, device_id_type=MESH,
        )

    def peer_arrival(h, c, i):
        s = slot(h)
        return pltpu.make_async_remote_copy(
            src_ref=place(s, c, i), dst_ref=place(s, c, i),
            send_sem=send_sem.at[s, c, i], recv_sem=recv_sem.at[s, c, i],
            device_id={"seq": c * 2 + core}, device_id_type=MESH,
        )

    def forward(h, half):
        s = slot(h)
        part = kv[s].at[pl.ds(half * 2 * chips * blk_dev, 2 * chips * blk_dev)]
        return pltpu.make_async_remote_copy(
            src_ref=part, dst_ref=part,
            send_sem=fsend.at[s], recv_sem=frecv.at[s],
            device_id={"seq": partner}, device_id_type=MESH,
        )

    def ship(src, dst, k):
        return pltpu.make_async_remote_copy(
            src_ref=src, dst_ref=dst, send_sem=ship_send.at[k], recv_sem=ship_recv.at[k],
            device_id={"segment": after}, device_id_type=MESH,
        )

    shipped = [ship(own_rows(moved, i), place(slots, chip, i), i) for i in range(2)]
    shipped += [ship(rand_hbm, rand_in, 2), ship(glob_hbm, glob_in, 3)]
    shipped.append(ship(q_ref.at[0, :, pl.ds(moved * gw, gw)], q_buf.at[moved], 4))
    list_copies = [
        pltpu.make_async_copy(rand_in, rand_moved, table_sem.at[0]),
        pltpu.make_async_copy(glob_in, glob_moved, table_sem.at[1]),
    ]

    def start_gather(h):
        if slots <= h < moved:
            pl.semaphore_wait(free_c.at[h % slots], chips - 1)
        for i in range(2):
            if h == moved:
                shipped[i].wait_recv()
            for c in others:
                peer_copy(h, c, i).start()
            if h < moved:
                own_copy(h, i).start()

    barrier = pltpu.get_barrier_semaphore()
    greeted = [{"seq": c * 2 + core} for c in others]
    greeted += [{"seq": partner}, {"segment": after}, {"segment": before}]
    for who in greeted:
        pl.semaphore_signal(barrier, inc=1, device_id=who, device_id_type=MESH)
    q_copy(0).start()
    pl.semaphore_wait(barrier, len(greeted))

    start_gather(0)
    for copy in shipped:
        copy.start()
    for h in range(1, ahead):
        start_gather(h)
    for h in range(1, moved):
        q_copy(h).start()

    scale = 1.0 / math.sqrt(HEAD)
    column = lax.broadcasted_iota(jnp.int32, (1, (3 + GLOB + RAND) * BLOCK), 1)

    for h in range(kvh):
        s = slot(h)
        for i in range(2):
            if h < moved:
                own_copy(h, i).wait()
            for c in others:
                peer_arrival(h, c, i).wait_recv()
        if slots <= h < moved:
            pl.semaphore_wait(free_p.at[s], 1)
        forward(h, core).start()
        if h + ahead < slots:
            start_gather(h + ahead)
        if h + ahead == moved:
            start_gather(moved)
        if h < moved:
            q_copy(h).wait()
        else:
            for arrival, copy in zip(shipped[2:4], list_copies):
                arrival.wait_recv()
                copy.start()
            for copy in list_copies:
                copy.wait()
            shipped[4].wait_recv()
        forward(h, 1 - core).wait_recv()

        def block_step(j, carry, h=h, s=s):
            rand, glob = (rand_ref, glob_ref) if h < moved else (rand_moved, glob_moved)
            row = me * blk_dev + j
            listed = [jnp.maximum(row - 1, 0), row, jnp.minimum(row + 1, nblk - 1)]
            listed += [glob[0, i] for i in range(GLOB)] + [rand[i, 0, j] for i in range(RAND)]

            def picked(i):
                parts = []
                for b in listed:
                    dev = lax.div(b, blk_dev)
                    where = (lax.rem(dev, 2) * 2 + i) * chips + lax.div(dev, 2)
                    parts.append(kv[s][where * blk_dev + lax.rem(b, blk_dev)])
                return jnp.concatenate(parts, axis=0)

            rows = pl.ds(pl.multiple_of(j * BLOCK, BLOCK), BLOCK)
            q_rows = q_buf[h, rows, :]
            q = jnp.concatenate([q_rows[:, g * HEAD : (g + 1) * HEAD] for g in range(group)], axis=0)
            scores = lax.dot_general(
                q, picked(0), (((1,), (1,)), ((), ())), preferred_element_type=jnp.float32
            )
            listed_here = ((column >= BLOCK) | (row >= 1)) & (
                (column < 2 * BLOCK) | (column >= 3 * BLOCK) | (row + 1 < nblk)
            )
            scores = scores * scale + jnp.where(listed_here, 0.0, -jnp.inf)
            top = jnp.max(scores, axis=-1, keepdims=True)
            expo = jnp.exp(scores - top)
            weights = (expo * (1.0 / jnp.sum(expo, axis=-1, keepdims=True))).astype(jnp.bfloat16)
            result = jnp.dot(weights, picked(1), preferred_element_type=jnp.float32)
            result = result.astype(jnp.bfloat16)
            for g in range(group):
                piece = result[g * BLOCK : (g + 1) * BLOCK, :]
                if h < moved:
                    res[h, rows, pl.ds(g * HEAD, HEAD)] = piece
                else:
                    out_ref[0, rows, pl.ds(h * gw + g * HEAD, HEAD)] = piece
            if h < moved:
                pltpu.make_async_remote_copy(
                    src_ref=res.at[h, rows, :],
                    dst_ref=out_ref.at[0, rows, pl.ds(h * gw, gw)],
                    send_sem=zsend.at[h], recv_sem=zrecv.at[h],
                    device_id={"segment": after}, device_id_type=MESH,
                ).start()
            return carry

        lax.fori_loop(0, blk_dev, block_step, 0)

        for i in range(2):
            for c in others:
                peer_copy(h, c, i).wait_send()
        forward(h, core).wait_send()
        if h + slots < moved:
            for c in others:
                pl.semaphore_signal(
                    free_c.at[s], inc=1, device_id={"seq": c * 2 + core}, device_id_type=MESH
                )
            pl.semaphore_signal(
                free_p.at[s], inc=1, device_id={"seq": partner}, device_id_type=MESH
            )
            start_gather(h + slots)

    for copy in shipped:
        copy.wait_send()
    for h in range(moved):
        pltpu.make_async_remote_copy(
            src_ref=res.at[h],
            dst_ref=out_ref.at[0, :, pl.ds(h * gw, gw)],
            send_sem=zsend.at[h], recv_sem=zrecv.at[h],
            device_id={"segment": after}, device_id_type=MESH,
        ).wait()


def per_device(queries, keys_in, values_in, random_blocks, global_blocks):
    n, segs = lax.axis_size("seq"), lax.axis_size("segment")
    tok, width = queries.shape[1:]
    kvh = keys_in.shape[2] // HEAD
    gw = width // kvh
    chips = n // 2
    blk_dev = tok // BLOCK
    slots = min(kvh - 1, max(2, SLOT_BYTES // (4 * n * tok * HEAD)))
    anywhere = pl.BlockSpec(memory_space=pl.ANY)
    scalars = pl.BlockSpec(memory_space=pltpu.SMEM)
    keys = (3 + GLOB + RAND) * BLOCK
    keys_in, values_in = (x.reshape(blk_dev, BLOCK, kvh * HEAD) for x in (keys_in, values_in))
    random_blocks = jnp.transpose(random_blocks, (2, 0, 1))
    return pl.pallas_call(
        functools.partial(kernel, n, segs, kvh, slots, min(2, slots)),
        out_shape=pltpu.VMEM(queries.shape, jnp.bfloat16),
        in_specs=[scalars] * 2 + [anywhere] * 5,
        out_specs=pl.BlockSpec(memory_space=pltpu.VMEM),
        scratch_shapes=[
            pltpu.VMEM((kvh, tok, gw), jnp.bfloat16),
            pltpu.VMEM((kvh - 1, tok, gw), jnp.bfloat16),
            pltpu.VMEM(random_blocks.shape, jnp.int32),
            pltpu.VMEM(global_blocks.shape, jnp.int32),
            pltpu.SMEM(random_blocks.shape, jnp.int32),
            pltpu.SMEM(global_blocks.shape, jnp.int32),
            *[
                pltpu.VMEM((4 * chips * blk_dev, BLOCK, HEAD), jnp.bfloat16)
                for _ in range(slots + 1)
            ],
            pltpu.SemaphoreType.DMA((kvh,)),
            pltpu.SemaphoreType.DMA((slots + 1, 2)),
            pltpu.SemaphoreType.DMA((slots + 1, chips, 2)),
            pltpu.SemaphoreType.DMA((slots + 1, chips, 2)),
            pltpu.SemaphoreType.DMA((slots + 1,)),
            pltpu.SemaphoreType.DMA((slots + 1,)),
            pltpu.SemaphoreType.DMA((kvh,)),
            pltpu.SemaphoreType.DMA((kvh,)),
            pltpu.SemaphoreType.DMA((5,)),
            pltpu.SemaphoreType.DMA((5,)),
            pltpu.SemaphoreType.DMA((2,)),
            pltpu.SemaphoreType.REGULAR((slots,)),
            pltpu.SemaphoreType.REGULAR((slots,)),
        ],
        compiler_params=pltpu.CompilerParams(
            collective_id=0, has_side_effects=True, vmem_limit_bytes=46 * 1024 * 1024
        ),
        cost_estimate=pl.CostEstimate(
            flops=4 * tok * width * keys,
            bytes_accessed=4 * tok * width,
            transcendentals=tok * width // HEAD * keys,
        ),
    )(random_blocks, global_blocks, random_blocks, global_blocks, queries, keys_in, values_in)


def solution(mesh):
    in_specs = (
        P("segment", "seq", None),
        P("segment", "seq", None),
        P("segment", "seq", None),
        P("segment", "seq", None),
        P("segment", None),
    )
    out_specs = P("segment", "seq", None)
    return jax.shard_map(
        per_device, mesh=mesh, in_specs=in_specs, out_specs=out_specs, check_vma=False
    )
```

time: 216 us -> 200 us (0.926)
  Pallas kernels: 205 us -> 196 us
  local copies, waits for them, and re-layouts: 9.12 us -> 3.4 us
    pallas_call x1, Pallas kernels: 205 us -> 196 us  [per_device(): pl.pallas_call(functools.partial(kernel, n, segs, kvh, slots, min(2, slot...]
    unnamed x2 -> x1, local copies, waits for them, and re-layouts: 9.12 us -> 3.4 us
where the time goes in v2:
time: 200 us
  Pallas kernels  196 us (98%)
  local copies, waits for them, and re-layouts  3.4 us (2%)
    pallas_call x1, Pallas kernels, per_device(): pl.pallas_call(functools.partial(kernel, n, segs, kvh, slots, min(2, slot...  196 us

profile of v2, /device:TPU:0, one launch (start us, length us, event | category | flops | bytes accessed | tf_op | source)
XLA Modules:
  0.0 199.6 jit_solution(16982093230765592217)
XLA Ops:
  0.0 196.1 %shard_map.55 = bf16[1,512,8192]{2,1,0:T(8,128)(2,1)S(1)} custom-call(s32[3,1,8]{2,1,0:T(1,128)} %bitcast.5, s32[1,2]{1,0:T(1,128)} %glob_hbm.1, s32[3,1,8]{2,1,0:T(1,128)} %bitcast.6, s32[1,2]{1,0:T(1,128)} %glob_hbm.1, bf16[1,512,8192]{2,1,0:T(8,128)(2,1)} %q_ref.1, bf16[8,64,1024]{2,1,0:T(8,128)(2,1)} %bitcast.3, bf16[8,64,1024]{2,1,0:T(8,128)(2,1)} %bitcast.4), custom_call_target="tpu_custom_call" | custom-call | flops 8589934592 | bytes 16777216 | tf_op jit(solution)/shard_map/pallas_call | solution.py:241
  196.2 3.4 %copy.7 = bf16[1,512,8192]{2,1,0:T(8,128)(2,1)} copy(bf16[1,512,8192]{2,1,0:T(8,128)(2,1)S(1)} %shard_map.55) | data formatting | bytes 16777216

commit v3 on v2

--- a/solution.py
+++ b/solution.py
@@ -118,10 +118,9 @@
     q_copy(0).start()
     pl.semaphore_wait(barrier, len(greeted))
 
-    start_gather(0)
     for copy in shipped:
         copy.start()
-    for h in range(1, ahead):
+    for h in range(ahead):
         start_gather(h)
     for h in range(1, moved):
         q_copy(h).start()
@@ -188,11 +187,11 @@
                 if h < moved:
                     res[h, rows, pl.ds(g * HEAD, HEAD)] = piece
                 else:
-                    out_ref[0, rows, pl.ds(h * gw + g * HEAD, HEAD)] = piece
+                    out_ref[h, rows, pl.ds(g * HEAD, HEAD)] = piece
             if h < moved:
                 pltpu.make_async_remote_copy(
                     src_ref=res.at[h, rows, :],
-                    dst_ref=out_ref.at[0, rows, pl.ds(h * gw, gw)],
+                    dst_ref=out_ref.at[h, rows, :],
                     send_sem=zsend.at[h], recv_sem=zrecv.at[h],
                     device_id={"segment": after}, device_id_type=MESH,
                 ).start()
@@ -219,10 +218,22 @@
     for h in range(moved):
         pltpu.make_async_remote_copy(
             src_ref=res.at[h],
-            dst_ref=out_ref.at[0, :, pl.ds(h * gw, gw)],
+            dst_ref=out_ref.at[h],
             send_sem=zsend.at[h], recv_sem=zrecv.at[h],
             device_id={"segment": after}, device_id_type=MESH,
         ).wait()
+
+
+def write_out(x_ref, out_ref, sems):
+    heads, _, gw = x_ref.shape
+    copies = [
+        pltpu.make_async_copy(x_ref.at[h], out_ref.at[0, :, pl.ds(h * gw, gw)], sems.at[h])
+        for h in range(heads)
+    ]
+    for copy in copies:
+        copy.start()
+    for copy in copies:
+        copy.wait()
 
 
 def per_device(queries, keys_in, values_in, random_blocks, global_blocks):
@@ -238,9 +249,9 @@
     keys = (3 + GLOB + RAND) * BLOCK
     keys_in, values_in = (x.reshape(blk_dev, BLOCK, kvh * HEAD) for x in (keys_in, values_in))
     random_blocks = jnp.transpose(random_blocks, (2, 0, 1))
-    return pl.pallas_call(
+    landed = pl.pallas_call(
         functools.partial(kernel, n, segs, kvh, slots, min(2, slots)),
-        out_shape=pltpu.VMEM(queries.shape, jnp.bfloat16),
+        out_shape=pltpu.VMEM((kvh, tok, gw), jnp.bfloat16),
         in_specs=[scalars] * 2 + [anywhere] * 5,
         out_specs=pl.BlockSpec(memory_space=pltpu.VMEM),
         scratch_shapes=[
@@ -277,6 +288,16 @@
             transcendentals=tok * width // HEAD * keys,
         ),
     )(random_blocks, global_blocks, random_blocks, global_blocks, queries, keys_in, values_in)
+    return pl.pallas_call(
+        write_out,
+        out_shape=jax.ShapeDtypeStruct(queries.shape, jnp.bfloat16),
+        in_specs=[pl.BlockSpec(memory_space=pltpu.VMEM)],
+        out_specs=anywhere,
+        scratch_shapes=[pltpu.SemaphoreType.DMA((kvh,))],
+        cost_estimate=pl.CostEstimate(
+            flops=0, bytes_accessed=2 * tok * width, transcendentals=0
+        ),
+    )(landed)
 
 
 def solution(mesh):

time: 200 us -> 206 us (1.030)
  Pallas kernels: 196 us -> 203 us
    pallas_call x0 -> x1, Pallas kernels: none -> 6.75 us  [per_device(): pl.pallas_call(write_out, out_shape=jax.ShapeDtypeStruct(queries.shape, j...]
where the time goes in v3:
time: 206 us
  Pallas kernels  203 us (99%)
  local copies, waits for them, and re-layouts  3.21 us (2%)
    pallas_call x1, Pallas kernels, per_device(): pl.pallas_call(functools.partial(kernel, n, segs, kvh, slots, min(2, slot...  196 us
    pallas_call x1, Pallas kernels, per_device(): pl.pallas_call(write_out, out_shape=jax.ShapeDtypeStruct(queries.shape, j...  6.75 us

profile of v3, /device:TPU:0, one launch (start us, length us, event | category | flops | bytes accessed | tf_op | source)
XLA Modules:
  0.0 206.1 jit_solution(14834507874889599153)
XLA Ops:
  0.0 196.1 %shard_map.55.x_ref = bf16[8,512,1024]{2,1,0:T(8,128)(2,1)S(1)} custom-call(s32[3,1,8]{2,1,0:T(1,128)} %bitcast.5, s32[1,2]{1,0:T(1,128)} %glob_hbm.1, s32[3,1,8]{2,1,0:T(1,128)} %bitcast.6, s32[1,2]{1,0:T(1,128)} %glob_hbm.1, bf16[1,512,8192]{2,1,0:T(8,128)(2,1)} %q_ref.1, bf16[8,64,1024]{2,1,0:T(8,128)(2,1)} %bitcast.3, bf16[8,64,1024]{2,1,0:T(8,128)(2,1)} %bitcast.4), custom_call_target="tpu_custom_call" | custom-call | flops 8589934592 | bytes 16777216 | tf_op jit(solution)/shard_map/pallas_call | solution.py:252
  196.1 0.0 copy-start
  196.2 3.2 %copy-done = bf16[8,512,1024]{2,1,0:T(8,128)(2,1)} copy-done((bf16[8,512,1024]{2,1,0:T(8,128)(2,1)}, bf16[8,512,1024]{2,1,0:T(8,128)(2,1)S(1)}, u32[]{:S(2)}) %copy-start) | copy-done | bytes 8388632
  199.4 6.7 %shard_map.56 = bf16[1,512,8192]{2,1,0:T(8,128)(2,1)} custom-call(bf16[8,512,1024]{2,1,0:T(8,128)(2,1)} %copy-done), custom_call_target="tpu_custom_call" | custom-call | bytes 8388608 | tf_op jit(solution)/shard_map/pallas_call | solution.py:291
Async XLA Ops:
  196.1 3.2 %copy-start = (bf16[8,512,1024]{2,1,0:T(8,128)(2,1)}, bf16[8,512,1024]{2,1,0:T(8,128)(2,1)S(1)}, u32[]{:S(2)}) copy-start(bf16[8,512,1024]{2,1,0:T(8,128)(2,1)S(1)} %shard_map.55.x_ref) | copy-start | bytes 25165828

commit v4 on v2

--- a/solution.py
+++ b/solution.py
@@ -99,6 +99,15 @@
         pltpu.make_async_copy(glob_in, glob_moved, table_sem.at[1]),
     ]
 
+    def hand_over(h, part, pieces):
+        rows = pl.ds(part * tok // pieces, tok // pieces)
+        return pltpu.make_async_remote_copy(
+            src_ref=res.at[h, rows, :],
+            dst_ref=out_ref.at[0, rows, pl.ds(h * gw, gw)],
+            send_sem=zsend.at[h], recv_sem=zrecv.at[h],
+            device_id={"segment": after}, device_id_type=MESH,
+        )
+
     def start_gather(h):
         if slots <= h < moved:
             pl.semaphore_wait(free_c.at[h % slots], chips - 1)
@@ -118,10 +127,9 @@
     q_copy(0).start()
     pl.semaphore_wait(barrier, len(greeted))
 
-    start_gather(0)
     for copy in shipped:
         copy.start()
-    for h in range(1, ahead):
+    for h in range(ahead):
         start_gather(h)
     for h in range(1, moved):
         q_copy(h).start()
@@ -189,16 +197,15 @@
                     res[h, rows, pl.ds(g * HEAD, HEAD)] = piece
                 else:
                     out_ref[0, rows, pl.ds(h * gw + g * HEAD, HEAD)] = piece
+            return carry
+
+        pieces = 2 if h == 0 else 1
+        for part in range(pieces):
+            lax.fori_loop(
+                part * blk_dev // pieces, (part + 1) * blk_dev // pieces, block_step, 0
+            )
             if h < moved:
-                pltpu.make_async_remote_copy(
-                    src_ref=res.at[h, rows, :],
-                    dst_ref=out_ref.at[0, rows, pl.ds(h * gw, gw)],
-                    send_sem=zsend.at[h], recv_sem=zrecv.at[h],
-                    device_id={"segment": after}, device_id_type=MESH,
-                ).start()
-            return carry
-
-        lax.fori_loop(0, blk_dev, block_step, 0)
+                hand_over(h, part, pieces).start()
 
         for i in range(2):
             for c in others:
@@ -217,12 +224,7 @@
     for copy in shipped:
         copy.wait_send()
     for h in range(moved):
-        pltpu.make_async_remote_copy(
-            src_ref=res.at[h],
-            dst_ref=out_ref.at[0, :, pl.ds(h * gw, gw)],
-            send_sem=zsend.at[h], recv_sem=zrecv.at[h],
-            device_id={"segment": after}, device_id_type=MESH,
-        ).wait()
+        hand_over(h, 0, 1).wait()
 
 
 def per_device(queries, keys_in, values_in, random_blocks, global_blocks):

time: 200 us -> 200 us (level)
  no operation moved by 1% of the time
where the time goes in v4:
time: 200 us
  Pallas kernels  196 us (98%)
  local copies, waits for them, and re-layouts  3.4 us (2%)
    pallas_call x1, Pallas kernels, per_device(): pl.pallas_call(functools.partial(kernel, n, segs, kvh, slots, min(2, slot...  196 us

profile of v4, /device:TPU:0, one launch (start us, length us, event | category | flops | bytes accessed | tf_op | source)
XLA Modules:
  0.0 199.5 jit_solution(8501847786286925677)
XLA Ops:
  0.0 196.1 %shard_map.55 = bf16[1,512,8192]{2,1,0:T(8,128)(2,1)S(1)} custom-call(s32[3,1,8]{2,1,0:T(1,128)} %bitcast.5, s32[1,2]{1,0:T(1,128)} %glob_hbm.1, s32[3,1,8]{2,1,0:T(1,128)} %bitcast.6, s32[1,2]{1,0:T(1,128)} %glob_hbm.1, bf16[1,512,8192]{2,1,0:T(8,128)(2,1)} %q_ref.1, bf16[8,64,1024]{2,1,0:T(8,128)(2,1)} %bitcast.3, bf16[8,64,1024]{2,1,0:T(8,128)(2,1)} %bitcast.4), custom_call_target="tpu_custom_call" | custom-call | flops 8589934592 | bytes 16777216 | tf_op jit(solution)/shard_map/pallas_call | solution.py:243
  196.1 3.4 %copy.7 = bf16[1,512,8192]{2,1,0:T(8,128)(2,1)} copy(bf16[1,512,8192]{2,1,0:T(8,128)(2,1)S(1)} %shard_map.55) | data formatting | bytes 16777216

commit v5 on v4

--- a/solution.py
+++ b/solution.py
@@ -13,6 +13,7 @@
 GLOB = 2
 RAND = 3
 MESH = pl.DeviceIdType.MESH
+PIECES = 8
 SLOT_BYTES = 16 * 1024 * 1024
 
 
@@ -227,6 +228,20 @@
         hand_over(h, 0, 1).wait()
 
 
+def write_out(x_ref, out_ref, sems):
+    rows = out_ref.shape[1] // PIECES
+    copies = [
+        pltpu.make_async_copy(
+            x_ref.at[:, pl.ds(i * rows, rows), :], out_ref.at[:, pl.ds(i * rows, rows), :], sems.at[i]
+        )
+        for i in range(PIECES)
+    ]
+    for copy in copies:
+        copy.start()
+    for copy in copies:
+        copy.wait()
+
+
 def per_device(queries, keys_in, values_in, random_blocks, global_blocks):
     n, segs = lax.axis_size("seq"), lax.axis_size("segment")
     tok, width = queries.shape[1:]
@@ -240,7 +255,7 @@
     keys = (3 + GLOB + RAND) * BLOCK
     keys_in, values_in = (x.reshape(blk_dev, BLOCK, kvh * HEAD) for x in (keys_in, values_in))
     random_blocks = jnp.transpose(random_blocks, (2, 0, 1))
-    return pl.pallas_call(
+    landed = pl.pallas_call(
         functools.partial(kernel, n, segs, kvh, slots, min(2, slots)),
         out_shape=pltpu.VMEM(queries.shape, jnp.bfloat16),
         in_specs=[scalars] * 2 + [anywhere] * 5,
@@ -279,6 +294,16 @@
             transcendentals=tok * width // HEAD * keys,
         ),
     )(random_blocks, global_blocks, random_blocks, global_blocks, queries, keys_in, values_in)
+    return pl.pallas_call(
+        write_out,
+        out_shape=pltpu.HBM(queries.shape, jnp.bfloat16),
+        in_specs=[pl.BlockSpec(memory_space=pltpu.VMEM)],
+        out_specs=pl.BlockSpec(memory_space=pltpu.HBM),
+        scratch_shapes=[pltpu.SemaphoreType.DMA((PIECES,))],
+        cost_estimate=pl.CostEstimate(
+            flops=0, bytes_accessed=2 * tok * width, transcendentals=0
+        ),
+    )(landed)
 
 
 def solution(mesh):

time: 200 us -> 206 us (1.030)
  Pallas kernels: 196 us -> 203 us
    pallas_call x0 -> x1, Pallas kernels: none -> 6.75 us  [per_device(): pl.pallas_call(write_out, out_shape=pltpu.HBM(queries.shape, jnp.bfloat16...]
where the time goes in v5:
time: 206 us
  Pallas kernels  203 us (99%)
  local copies, waits for them, and re-layouts  3.21 us (2%)
    pallas_call x1, Pallas kernels, per_device(): pl.pallas_call(functools.partial(kernel, n, segs, kvh, slots, min(2, slot...  196 us
    pallas_call x1, Pallas kernels, per_device(): pl.pallas_call(write_out, out_shape=pltpu.HBM(queries.shape, jnp.bfloat16...  6.75 us

profile of v5, /device:TPU:0, one launch (start us, length us, event | category | flops | bytes accessed | tf_op | source)
XLA Modules:
  0.0 206.1 jit_solution(17682631282345674039)
XLA Ops:
  0.0 196.1 %shard_map.55.x_ref = bf16[1,512,8192]{2,1,0:T(8,128)(2,1)S(1)} custom-call(s32[3,1,8]{2,1,0:T(1,128)} %bitcast.5, s32[1,2]{1,0:T(1,128)} %glob_hbm.1, s32[3,1,8]{2,1,0:T(1,128)} %bitcast.6, s32[1,2]{1,0:T(1,128)} %glob_hbm.1, bf16[1,512,8192]{2,1,0:T(8,128)(2,1)} %q_ref.1, bf16[8,64,1024]{2,1,0:T(8,128)(2,1)} %bitcast.3, bf16[8,64,1024]{2,1,0:T(8,128)(2,1)} %bitcast.4), custom_call_target="tpu_custom_call" | custom-call | flops 8589934592 | bytes 16777216 | tf_op jit(solution)/shard_map/pallas_call | solution.py:258
  196.1 0.0 copy-start
  196.2 3.2 %copy-done = bf16[1,512,8192]{2,1,0:T(8,128)(2,1)} copy-done((bf16[1,512,8192]{2,1,0:T(8,128)(2,1)}, bf16[1,512,8192]{2,1,0:T(8,128)(2,1)S(1)}, u32[]{:S(2)}) %copy-start) | copy-done | bytes 8388632
  199.4 6.7 %shard_map.56 = bf16[1,512,8192]{2,1,0:T(8,128)(2,1)} custom-call(bf16[1,512,8192]{2,1,0:T(8,128)(2,1)} %copy-done), custom_call_target="tpu_custom_call" | custom-call | bytes 8388608 | tf_op jit(solution)/shard_map/pallas_call | solution.py:297
Async XLA Ops:
  196.1 3.2 %copy-start = (bf16[1,512,8192]{2,1,0:T(8,128)(2,1)}, bf16[1,512,8192]{2,1,0:T(8,128)(2,1)S(1)}, u32[]{:S(2)}) copy-start(bf16[1,512,8192]{2,1,0:T(8,128)(2,1)S(1)} %shard_map.55.x_ref) | copy-start | bytes 25165828

commit v6 on v5

--- a/solution.py
+++ b/solution.py
@@ -300,10 +300,11 @@
         in_specs=[pl.BlockSpec(memory_space=pltpu.VMEM)],
         out_specs=pl.BlockSpec(memory_space=pltpu.HBM),
         scratch_shapes=[pltpu.SemaphoreType.DMA((PIECES,))],
+        compiler_params=pltpu.CompilerParams(vmem_limit_bytes=16 * 1024 * 1024),
         cost_estimate=pl.CostEstimate(
             flops=0, bytes_accessed=2 * tok * width, transcendentals=0
         ),
-    )(landed)
+    )(pltpu.with_memory_space_constraint(landed, pltpu.VMEM))
 
 
 def solution(mesh):

time: 206 us -> 200 us (0.971)
  local copies, waits for them, and re-layouts: 3.21 us -> 0 us
  Pallas kernels: 203 us -> 200 us
    pallas_call x1, Pallas kernels: 6.75 us -> 3.37 us  [per_device(): pl.pallas_call(write_out, out_shape=pltpu.HBM(queries.shape, jnp.bfloat16...]
    unnamed x2 -> x0, local copies, waits for them, and re-layouts: 3.21 us -> none
where the time goes in v6:
time: 200 us
  Pallas kernels  200 us (100%)
    pallas_call x1, Pallas kernels, per_device(): pl.pallas_call(functools.partial(kernel, n, segs, kvh, slots, min(2, slot...  196 us

profile of v6, /device:TPU:0, one launch (start us, length us, event | category | flops | bytes accessed | tf_op | source)
XLA Modules:
  0.0 199.5 jit_solution(1733219060350945396)
XLA Ops:
  0.0 196.1 %shard_map.55.x_ref = bf16[1,512,8192]{2,1,0:T(8,128)(2,1)S(1)} custom-call(s32[3,1,8]{2,1,0:T(1,128)} %bitcast.5, s32[1,2]{1,0:T(1,128)} %glob_hbm.1, s32[3,1,8]{2,1,0:T(1,128)} %bitcast.6, s32[1,2]{1,0:T(1,128)} %glob_hbm.1, bf16[1,512,8192]{2,1,0:T(8,128)(2,1)} %q_ref.1, bf16[8,64,1024]{2,1,0:T(8,128)(2,1)} %bitcast.3, bf16[8,64,1024]{2,1,0:T(8,128)(2,1)} %bitcast.4), custom_call_target="tpu_custom_call" | custom-call | flops 8589934592 | bytes 16777216 | tf_op jit(solution)/shard_map/pallas_call | solution.py:258
  196.1 3.4 %shard_map.56 = bf16[1,512,8192]{2,1,0:T(8,128)(2,1)} custom-call(bf16[1,512,8192]{2,1,0:T(8,128)(2,1)S(1)} %shard_map.55.x_ref), custom_call_target="tpu_custom_call" | custom-call | bytes 8388608 | tf_op jit(solution)/shard_map/pallas_call | solution.py:297
